TPU v7x, 512 devices: a whole 4x4x16 slice. The times are simulated.
512 devices in a mesh: batch: 8 (over y, core), seq: 64 (over z, x).
Axes of the slice: x: 4, y: 4, z: 16, core: 2. Of those that a mesh axis runs over, the one named last changes fastest.
Arguments:
- queries: bfloat16 [131072, 1024], P(('batch', 'seq')), parts along dimension 0, may hold values from -12 to 12
- keys_values: bfloat16 [2, 131072, 1024], P(None, ('batch', 'seq')), parts along dimension 1, may hold values from -6 to 6
- random_blocks: int32 [2048, 16, 3], P(('batch', 'seq')), parts along dimension 0, may hold values from 0 to 255, as said below
- global_blocks: int32 [16], P('batch'), parts along dimension 0, may hold values from 0 to 255, as said below
- out_proj: bfloat16 [1024, 1024], P('seq'), may hold values from -0.375 to 0.375
Outputs:
- attended: bfloat16 [131072, 1024], P(('batch', 'seq')), parts along dimension 0
There are 8 independent parts, one for each index of `batch`. A program takes and returns all parts, laid end to end along the dimension named above; an argument that names none is the same for every part. Nothing has to cross between parts.
Inputs may be any that keep to these rules, and one draw needn't show every extreme that they name: Each list random_blocks[i, h] names 3 different blocks. Device d holds blocks d * 4 to (d + 1) * 4 - 1. Among the 64 lists of one device's query blocks no block is named more than 2 times and some block exactly 2 times; the blocks of any one device are named at most 6 times in all and those of some device exactly 6 times. The 2 global blocks are different; the last of them, global_blocks[1], is the sequence's last block 255.
All inputs are finite; a program needn't handle non-finite values.
Results may differ from a plain program's by a relative error of at most 0.0052.
Values may be sent and summed in bfloat16 or wider, within the bound.
A program may use at most 192 MiB of HBM per device.

v0:
```python
import jax
import jax.numpy as jnp
from jax import lax
from jax.sharding import PartitionSpec as P

H = 16
BLK = 64
R = 3


masked_score = -1e30


def padded_2(shard, sides, width):
    for axis, dim in sides:
        size, length = (lax.axis_size(axis), shard.shape[dim])
        up = [(i, (i + 1) % size) for i in range(size - 1)]
        down = [(j, i) for i, j in up]
        last = lax.slice_in_dim(shard, length - width, length, axis=dim)
        leading = lax.slice_in_dim(shard, 0, width, axis=dim)
        before = lax.ppermute(last, axis, up)
        after = lax.ppermute(leading, axis, down)
        shard = jnp.concatenate([before, shard, after], axis=dim)
    return shard


def broadcast(value, axis, source):
    kept = jnp.where(lax.axis_index(axis) == source, value, 0).astype(value.dtype)
    return lax.psum(kept, axis)


def slot_ranks(block_list):
    entries = block_list.shape[-1]
    position = jnp.arange(entries, dtype=jnp.int32)
    earlier_same = (block_list[..., :, None] == block_list[..., None, :]) & (
        position[None, :] < position[:, None]
    )
    return jnp.sum(earlier_same.astype(jnp.int32), axis=-1)


def per_device(queries, keys_values, random_blocks, global_blocks, out_proj):
    tokens = queries.shape[0]
    model_width = queries.shape[1]
    head_dim = model_width // H
    blocks_here = tokens // BLK
    devices = lax.axis_size("seq")
    my_index = lax.axis_index("seq")
    entries = blocks_here * H * R
    hot_owners = max(R, devices // 2)
    peer_most = (entries + hot_owners - 1) // hot_owners
    slot_count = (peer_most + blocks_here - 1) // blocks_here
    score_scale = head_dim ** (-0.5)
    glob_count = global_blocks.shape[0]
    block_ids = random_blocks.reshape(entries)
    head_ids = jnp.arange(entries, dtype=jnp.int32) // R % H
    owner_ids = block_ids // blocks_here
    capacity = blocks_here * slot_count
    within = block_ids % blocks_here * slot_count + slot_ranks(block_ids)
    slot_index = owner_ids * capacity + within
    marks_here = block_ids % blocks_here * H + head_ids + 1
    request = jnp.zeros((devices * capacity,), jnp.int32).at[slot_index].set(marks_here)
    incoming = lax.all_to_all(
        request.reshape(devices, capacity), "seq", split_axis=0, concat_axis=0, tiled=True
    )
    kv_table = keys_values.reshape(2, blocks_here, BLK, H, head_dim).transpose(0, 1, 3, 2, 4)
    kv_table = kv_table.reshape(2, blocks_here * H, BLK * head_dim)
    wanted = jnp.maximum(incoming - 1, 0)
    outgoing = jnp.take(kv_table, wanted.reshape(-1), axis=1).reshape(
        2, devices, capacity, BLK * head_dim
    )
    returned = lax.all_to_all(outgoing, "seq", split_axis=1, concat_axis=1, tiled=True)
    returned = returned.reshape(2, devices * capacity, BLK * head_dim)
    picked = jnp.take(returned, slot_index, axis=1).reshape(2, blocks_here, H, R * BLK, head_dim)
    padded = padded_2(keys_values, (("seq", 1),), BLK)
    query_list = []
    kv_list = []
    for glob_slot in range(glob_count):
        chosen = global_blocks[glob_slot]
        local_start = chosen % blocks_here * BLK
        owner_index = chosen // blocks_here
        query_part = lax.dynamic_slice_in_dim(queries, local_start, BLK, 0)
        kv_part = lax.dynamic_slice_in_dim(keys_values, local_start, BLK, 1)
        sent_query, sent_kv = (
            broadcast(query_part, "seq", owner_index),
            broadcast(kv_part, "seq", owner_index),
        )
        query_list.append(sent_query)
        kv_list.append(sent_kv)
    glob_query = jnp.concatenate(query_list, axis=0).reshape(glob_count * BLK, H, head_dim)
    glob_kv = jnp.concatenate(kv_list, axis=1).reshape(2, glob_count * BLK, H, head_dim)
    local_keys = keys_values[0].reshape(tokens, H, head_dim)
    glob_scores = (
        jnp.einsum("qhd,khd->hqk", glob_query, local_keys, preferred_element_type=jnp.float32)
        * score_scale
    )
    local_max = jnp.max(glob_scores, axis=2)
    values_wide = keys_values[1].astype(jnp.float32).reshape(tokens, H, head_dim)
    row_max = lax.pmax(local_max, "seq")
    weights = jnp.exp(glob_scores - row_max[:, :, None])
    weighted = jnp.einsum("hqk,khd->hdq", weights, values_wide, precision=lax.Precision.HIGHEST)
    local_sum = jnp.sum(weights, axis=2)
    glob_sum, glob_acc = lax.psum((local_sum, weighted), "seq")
    glob_ctx = (
        (glob_acc / glob_sum[:, None, :]).transpose(2, 0, 1).reshape(glob_count, BLK, model_width)
    )
    glob_ctx = glob_ctx.astype(jnp.bfloat16)
    query_blocks = queries.reshape(blocks_here, BLK, H, head_dim)
    first_dev = my_index == 0
    last_dev = my_index == devices - 1
    key_block_pos = jnp.arange(3 * BLK, dtype=jnp.int32) // BLK

    def attend(block_index):
        qblock = lax.dynamic_index_in_dim(query_blocks, block_index, 0, keepdims=False)
        window = lax.dynamic_slice_in_dim(padded, block_index * BLK, 3 * BLK, 1).reshape(
            2, 3 * BLK, H, head_dim
        )
        rand_kv = lax.dynamic_index_in_dim(picked, block_index, 1, keepdims=False)
        win_scores = jnp.einsum(
            "qhd,khd->hqk", qblock, window[0], preferred_element_type=jnp.float32
        )
        side_scores = jnp.einsum(
            "qhd,khd->hqk", qblock, glob_kv[0], preferred_element_type=jnp.float32
        )
        rand_scores = jnp.einsum(
            "qhd,hkd->hqk", qblock, rand_kv[0], preferred_element_type=jnp.float32
        )
        scores = jnp.concatenate([win_scores, side_scores, rand_scores], axis=2) * score_scale
        left_bad = first_dev & (block_index == 0)
        right_bad = last_dev & (block_index == blocks_here - 1)
        invalid = (key_block_pos == 0) & left_bad | (key_block_pos == 2) & right_bad
        keep_mask = jnp.concatenate([~invalid, jnp.ones((glob_count * BLK + R * BLK,), bool)])
        scores = jnp.where(keep_mask[None, None, :], scores, masked_score)
        row_max = jnp.max(scores, axis=2)
        weights = jnp.exp(scores - row_max[:, :, None])
        totals = jnp.sum(weights, axis=2)
        rounded = weights.astype(jnp.bfloat16)
        split_one = 3 * BLK
        split_two = 3 * BLK + glob_count * BLK
        mixed = jnp.einsum(
            "hqk,khd->qhd", rounded[:, :, :split_one], window[1], preferred_element_type=jnp.float32
        )
        mixed = mixed + jnp.einsum(
            "hqk,khd->qhd",
            rounded[:, :, split_one:split_two],
            glob_kv[1],
            preferred_element_type=jnp.float32,
        )
        mixed = mixed + jnp.einsum(
            "hqk,hkd->qhd",
            rounded[:, :, split_two:],
            rand_kv[1],
            preferred_element_type=jnp.float32,
        )
        return (mixed / totals.T[:, :, None]).astype(jnp.bfloat16).reshape(BLK, model_width)

    context = lax.map(attend, jnp.arange(blocks_here, dtype=jnp.int32))
    here_ids = my_index * blocks_here + jnp.arange(blocks_here, dtype=jnp.int32)
    for glob_slot in range(glob_count):
        matches = here_ids == global_blocks[glob_slot]
        context = jnp.where(matches[:, None, None], glob_ctx[glob_slot][None], context)
    flat_context = context.reshape(tokens, model_width)
    result = jnp.dot(
        flat_context,
        lax.all_gather(out_proj, "seq", axis=0, tiled=True),
        preferred_element_type=jnp.float32,
    )
    return result.astype(jnp.bfloat16)


def solution(mesh):
    placed = (
        P(("batch", "seq"), None),
        P(None, ("batch", "seq"), None),
        P(("batch", "seq"), None, None),
        P("batch"),
        P("seq", None),
    )
    return jax.shard_map(
        per_device, mesh=mesh, in_specs=placed, out_specs=P(("batch", "seq"), None), check_vma=False
    )
```

profile of v0, /device:TPU:24, one launch (start us, length us, event | category | flops | bytes accessed | tf_op | source)
XLA Modules:
  0.0 1047.1 jit_solution(12267629278336123860)
XLA Ops:
  9.7 18.6 %all-to-all-start = ((s32[64,1,8]{2,1,0:T(1,128)}), s32[64,1,8]{2,1,0:T(1,128)S(1)}, u32[]{:S(2)}, u32[]{:S(2)}) async-start(s32[64,1,8]{2,1,0:T(1,128)} %bitcast.12), calls=%async_computation | async-start | bytes 65536 | tf_op jit(solution)/shard_map/all_to_all | solution.py:62
  28.3 4.0 reshape.240
  37.2 5.6 all-to-all-done
  43.2 25.9 %gather_fusion = bf16[512,2,4096]{2,1,0:T(2,128)(2,1)} fusion(bf16[2,64,4096]{2,0,1:T(2,128)(2,1)S(1)} %copy.110, s32[1024]{0:T(1024)S(1)} %pad_clamp_fusion.1), kind=kCustom, calls=%fused_computation | custom fusion | bytes 16779264 | tf_op jit(solution)/shard_map/jit(_take)/gather | solution.py:68
  69.1 11.4 %broadcast_select_fusion = bf16[2,64,8,4096]{3,0,2,1:T(2,128)(2,1)} fusion(bf16[2,64,8,4096]{3,0,2,1:T(2,128)(2,1)} %bitcast.109, pred[64,8]{1,0:T(8,128)(4,1)S(1)} %copy.107), kind=kLoop, calls=%fused_computation.42 | loop fusion | flops 4194304 | bytes 16777728 | tf_op jit(solution)/shard_map/jit(_take)/select_n | solution.py:68
  80.5 9.8 all-to-all-start.1
  100.1 379.7 %all-reduce.7.cloned.1.call-done = (bf16[2,64,1024]{2,1,0:T(8,128)(2,1)}, bf16[2,64,1024]{2,1,0:T(8,128)(2,1)}, bf16[64,1024]{1,0:T(8,128)(2,1)}, bf16[64,1024]{1,0:T(8,128)(2,1)}) async-done(((bf16[2,64,1024]{2,1,0:T(8,128)(2,1)}, bf16[2,64,1024]{2,1,0:T(8,128)(2,1)}, bf16[64,1024]{1,0:T(8,128)(2,1)}, bf16[64,1024]{1,0:T(8,128)(2,1)}), (bf16[2,64,1024]{2,1,0:T(8,128)(2,1)}, bf16[2,64,1024]{2,1,0:T(8,128)(2,1)}, ...) | async-done | bytes 786448 | tf_op jit(solution)/shard_map/psum | solution.py:29
  482.6 148.5 %pmax.7 = f32[16,128]{1,0:T(8,128)S(1)} all-reduce(f32[16,128]{1,0:T(8,128)S(1)} %get-tuple-element.180), channel_id=1, replica_groups=mesh['batch'=8,'seq'=64] {'seq'}, use_global_device_ids=true, to_apply=%region_3.4 | all-reduce | flops 2048 | bytes 16384 | tf_op jit(solution)/shard_map/pmax | solution.py:98
  631.1 3.5 fusion.27
  636.0 2.6 fusion.53
  638.6 4.0 collective-permute-start
  644.1 2.5 reshape.236
  649.8 5.0 collective-permute-done.1
  658.8 2.3 fusion.25
  661.1 140.1 %psum.45 = f32[16,128]{1,0:T(8,128)S(1)} all-reduce(f32[16,128]{1,0:T(8,128)S(1)} %fusion.25), channel_id=1, replica_groups=mesh['batch'=8,'seq'=64] {'seq'}, use_global_device_ids=true, to_apply=%region_6.7 | all-reduce | flops 2048 | bytes 16384 | tf_op jit(solution)/shard_map/psum | solution.py:102
  801.2 97.6 %all-reduce.5.cloned.1.call-done = f32[16,64,128]{2,1,0:T(8,128)} async-done(((f32[16,64,128]{2,1,0:T(8,128)}), f32[16,64,128]{2,1,0:T(8,128)}) %all-reduce.5.cloned.1.call-update) | async-done | bytes 524304 | tf_op jit(solution)/shard_map/psum | solution.py:102
  900.4 14.4 %gather_fusion.1 = bf16[192,2,4096]{2,1,0:T(2,128)(2,1)} fusion(bf16[2,512,4096]{2,0,1:T(2,128)(2,1)} %bitcast.17, s32[1024]{0:T(1024)S(1)} %pad_clamp_fusion), kind=kCustom, calls=%fused_computation.1 | custom fusion | bytes 6292224 | tf_op jit(solution)/shard_map/jit(_take)/gather | solution.py:73
  914.8 5.7 copy.111
  920.5 9.6 gather.15
  930.2 7.8 broadcast_select_fusion.1
  937.9 8.1 copy.113
  946.0 82.8 %while.12 = (s32[]{:T(128)}, bf16[4,64,1024]{2,1,0:T(8,128)(2,1)}, s32[4]{0:T(128)S(1)}, bf16[2,384,1024]{1,2,0:T(8,128)(2,1)S(1)}, pred[]{:T(512)}, /*index=5*/...) while((s32[]{:T(128)}, bf16[4,64,1024]{2,1,0:T(8,128)(2,1)}, ...), condition=%wide.region_14.15_spmd.clone.clone, body=%wide.region_11.14_spmd.clone.clone.sunk | while | flops 138153088 | bytes 20986124 | solution.py:156
  951.9 2.4 fusion.82
  956.7 7.2 fusion.85
  972.6 2.4 fusion.82
  977.4 7.2 fusion.85
  993.3 2.4 fusion.82
  998.1 7.2 fusion.85
  1014.0 2.4 fusion.82
  1018.8 7.2 fusion.85
  1030.0 7.5 all-gather.2.cloned.1.call-done
  1037.5 3.1 convolution_convert_fusion
  (141 shorter events, 57.5 us)
Async XLA Ops:
  9.7 33.1 %all-to-all-start = ((s32[64,1,8]{2,1,0:T(1,128)}), s32[64,1,8]{2,1,0:T(1,128)S(1)}, u32[]{:S(2)}, u32[]{:S(2)}) async-start(s32[64,1,8]{2,1,0:T(1,128)} %bitcast.12), calls=%async_computation | async-start | bytes 65536 | tf_op jit(solution)/shard_map/all_to_all | solution.py:62
  80.5 9.9 copy-start.9
  80.5 15.6 %copy-start.6 = (bf16[256,1024]{1,0:T(8,128)(2,1)S(1)}, bf16[256,1024]{1,0:T(8,128)(2,1)}, u32[]{:S(2)}) copy-start(bf16[256,1024]{1,0:T(8,128)(2,1)} %param.7) | copy-start | bytes 1572868
  80.5 16.4 %copy-start.2 = (bf16[2,256,1024]{2,1,0:T(8,128)(2,1)S(1)}, bf16[2,256,1024]{2,1,0:T(8,128)(2,1)}, u32[]{:S(2)}) copy-start(bf16[2,256,1024]{2,1,0:T(8,128)(2,1)} %param.8) | copy-start | bytes 3145732
  80.5 819.9 %all-to-all-start.1 = ((bf16[2,64,8,4096]{3,0,2,1:T(2,128)(2,1)}), bf16[2,64,8,4096]{3,0,2,1:T(2,128)(2,1)}, u32[]{:S(2)}, u32[]{:S(2)}) async-start(bf16[2,64,8,4096]{3,0,2,1:T(2,128)(2,1)} %broadcast_select_fusion), calls=%async_computation.1 | async-start | bytes 16777216 | tf_op jit(solution)/shard_map/all_to_all | solution.py:71
  90.3 389.5 %all-reduce.7.cloned.1.call-start = ((), (), s32[]{:S(2)}) async-start(), calls=%async_computation.4 | async-start | bytes 1572864 | tf_op jit(solution)/shard_map/psum | solution.py:29
  97.8 801.1 %all-reduce.5.cloned.1.call-start = ((), (), s32[]{:S(2)}) async-start(), calls=%async_computation.2 | async-start | bytes 1048576 | tf_op jit(solution)/shard_map/psum | solution.py:102
  482.6 153.4 %copy-start.1 = (f32[16,128,256]{2,1,0:T(8,128)}, f32[16,128,256]{2,1,0:T(8,128)S(1)}, u32[]{:S(2)}) copy-start(f32[16,128,256]{2,1,0:T(8,128)S(1)} %get-tuple-element.181) | copy-start | bytes 6291460
  634.6 9.4 copy-start.8
  634.7 402.8 %all-gather.2.cloned.1.call-start = ((), (), s32[]{:S(2)}) async-start(), calls=%async_computation.3 | async-start | bytes 2129920 | tf_op jit(solution)/shard_map/all_gather | solution.py:164
  636.0 18.7 %copy-start.3 = (bf16[2,256,1024]{1,2,0:T(8,128)(2,1)S(1)}, bf16[2,256,1024]{1,2,0:T(8,128)(2,1)}, u32[]{:S(2)}) copy-start(bf16[2,256,1024]{1,2,0:T(8,128)(2,1)} %copy.97) | copy-start | bytes 3145732
  638.6 11.2 %collective-permute-start = (bf16[2,64,1024]{1,2,0:T(8,128)(2,1)}, bf16[2,64,1024]{1,2,0:T(8,128)(2,1)S(1)}, u32[]{:S(2)}, u32[]{:S(2)}) collective-permute-start(bf16[2,64,1024]{1,2,0:T(8,128)(2,1)} %get-tuple-element.172), channel_id=1, source_target_pairs={{0,1},{1,2},{2,3},{3,4},{4,5},{5,6},{6,7},{7,8},{8,9},{9,10},{10,1... | collective-permute-start | bytes 786440 | tf_op jit(solution)/shard_map/ppermute | solution.py:21
  642.5 12.2 %collective-permute-start.1 = (bf16[2,64,1024]{1,2,0:T(8,128)(2,1)}, bf16[2,64,1024]{1,2,0:T(8,128)(2,1)}, u32[]{:S(2)}, u32[]{:S(2)}) collective-permute-start(bf16[2,64,1024]{1,2,0:T(8,128)(2,1)} %get-tuple-element.173), channel_id=1, source_target_pairs={{1,0},{2,1},{3,2},{4,3},{5,4},{6,5},{7,6},{8,7},{9,8},{10,9},{11,1... | collective-permute-start | bytes 786440 | tf_op jit(solution)/shard_map/ppermute | solution.py:22
  646.6 10.2 copy-start.7
  949.6 4.7 copy-start.4
  951.9 4.7 copy-start
  963.9 1.7 copy-start.5
  970.3 4.7 copy-start.4
  972.6 4.7 copy-start
  984.6 1.7 copy-start.5
  991.0 4.7 copy-start.4
  993.3 4.7 copy-start
  1005.3 1.7 copy-start.5
  1011.7 4.7 copy-start.4
  1014.0 4.7 copy-start
  1025.9 1.7 copy-start.5
Sparse Core Ops, SparseCore 0:
  97.9 381.8 all-reduce.6
  634.8 264.0 all-reduce.4
  901.8 135.6 all-gather.1
where the time goes:
time: 1050 us
  waiting for transfers between devices  497 us (47%)
  blocking collectives  289 us (28%)
  local copies, waits for them, and re-layouts  98.8 us (9%)
  other arithmetic  59.6 us (6%)
  matrix products  35.1 us (3%)
  starting transfers between devices  33.9 us (3%)
  between operations  18.5 us (2%)
  loops' own time  15.7 us (1%)
    psum x1, waiting for transfers between devices, broadcast(): return lax.psum(kept, axis)  380 us
    pmax x1, blocking collectives, per_device(): row_max = lax.pmax(local_max, 'seq')  149 us
    psum x1, blocking collectives, per_device(): glob_sum, glob_acc = lax.psum((local_sum, weighted), 'seq')  140 us
    psum x1, waiting for transfers between devices, per_device(): glob_sum, glob_acc = lax.psum((local_sum, weighted), 'seq')  97.6 us
    gather x3, local copies, waits for them, and re-layouts, per_device(): jnp.take(returned, slot_index, axis=1)  29.8 us
    sub x4, other arithmetic, attend(): weights = jnp.exp(scores - row_max[:, :, None])  28.7 us
    gather x1, local copies, waits for them, and re-layouts, per_device(): jnp.take(kv_table, wanted.reshape(-1), axis=1)  25.9 us
  transfers between devices with their start and end apart: 7, of which 6 were waited for; matrix products, arithmetic and copies ran while one was open for 14% of the time, Pallas kernels for 0%

commit v1 on v0

v1 whole, which is shorter than its diff:
```python
import functools

import jax
import jax.numpy as jnp
from jax import lax
from jax.experimental import pallas as pl
from jax.experimental.pallas import tpu as pltpu
from jax.sharding import PartitionSpec as P

H = 16
BLK = 64
R = 3
X = 4
G = 2
HALF = 64
LANES = 128
MESH = pl.DeviceIdType.MESH
NEG = -1e30
F32 = jnp.float32
BF16 = jnp.bfloat16


def swap(x):
    return pltpu.roll(x.astype(F32), HALF, 1).astype(x.dtype)


def dot_nt(a, b):
    return lax.dot_general(a, b, (((1,), (1,)), ((), ())), preferred_element_type=F32)


def dot_nn(a, b):
    return lax.dot_general(a, b, (((1,), (0,)), ((), ())), preferred_element_type=F32)


def kernel(
    nz, bd, scale2,
    gb_ref, q_ref, kv_ref, rb_ref, ctx_ref,
    qpack, kvpack, kvf, q_in, rb_in, rb_s, qc_in, gpart, gout, gkv, o_pack, o_in, stat,
    q_send, q_recv, rb_send, rb_recv, kv_send, kv_recv, o_send, o_recv,
    r_send, l_send, fl_recv, fr_recv, ha_send, hb_send, oa_recv, ob_recv,
    qc_send, qc_recv, gp_send, gp_recv, rbs_sem,
):
    tok = bd * BLK
    half_tok = tok // 2
    half_bd = bd // 2
    nb = nz * X * bd
    batch = lax.axis_index("batch")
    me = lax.axis_index("seq")
    z = me // X
    x = lax.rem(me, X)
    right = lax.rem(x + 1, X)
    left = lax.rem(x + X - 1, X)

    def dev(zz, xx):
        return (batch, zz * X + xx)

    def remote(src, dst, send, recv, where):
        return pltpu.make_async_remote_copy(
            src_ref=src, dst_ref=dst, send_sem=send, recv_sem=recv, device_id=where, device_id_type=MESH
        )

    def order(i):
        return lax.rem(jnp.where(lax.rem(i, 2) == 1, (i + 1) // 2, nz - i // 2), nz)

    def dest_of(i):
        return lax.rem(z + order(i), nz)

    def src_of(i):
        return lax.rem(z + nz - order(i), nz)

    def rows(zz, xx, first=0, count=None):
        return pl.ds(1 + (zz * X + xx) * bd + first, bd if count is None else count)

    barrier = pltpu.get_barrier_semaphore()

    @pl.loop(1, nz)
    def _(i):
        pl.semaphore_signal(barrier, inc=1, device_id=dev(lax.rem(z + i, nz), x), device_id_type=MESH)

    for d in range(1, X):
        pl.semaphore_signal(barrier, inc=1, device_id=dev(z, lax.rem(x + d, X)), device_id_type=MESH)

    lo_q = lax.broadcasted_iota(jnp.int32, (half_tok, LANES), 1) < HALF
    for p in range(nz // 2):
        cols = slice(p * LANES, (p + 1) * LANES)
        top, bot = q_ref[:half_tok, cols], q_ref[half_tok:, cols]
        qpack[2 * p] = jnp.where(lo_q, top, swap(bot)).reshape(half_bd, BLK, LANES)
        qpack[2 * p + 1] = jnp.where(lo_q, swap(top), bot).reshape(half_bd, BLK, LANES)

    pl.semaphore_wait(barrier, nz - 1 + X - 1)

    def q_copy(dz):
        return remote(qpack.at[dz], q_in.at[z], q_send.at[dz], q_recv.at[z], dev(dz, x))

    def rb_copy(dz):
        return remote(rb_ref.at[dz], rb_in.at[z], rb_send.at[dz], rb_recv.at[z], dev(dz, x))

    def kv_copy(dz):
        return remote(kvpack.at[dz], kvf.at[rows(z, x)], kv_send.at[dz], kv_recv.at[z], dev(dz, x))

    def o_copy(dz):
        return remote(o_pack.at[dz], o_in.at[z], o_send.at[dz], o_recv.at[z], dev(dz, x))

    @pl.loop(1, nz)
    def _(i):
        dz = dest_of(i)
        q_copy(dz).start()
        rb_copy(dz).start()

    lo_t = lax.broadcasted_iota(jnp.int32, (tok, LANES), 1) < HALF
    for p in range(nz // 2):
        cols = slice(p * LANES, (p + 1) * LANES)
        keys, vals = kv_ref[0, :, cols], kv_ref[1, :, cols]
        kvpack[2 * p] = jnp.where(lo_t, keys, swap(vals)).reshape(bd, BLK, LANES)
        kvpack[2 * p + 1] = jnp.where(lo_t, swap(keys), vals).reshape(bd, BLK, LANES)

    @pl.loop(1, nz)
    def _(i):
        kv_copy(dest_of(i)).start()

    q_in[z] = qpack[z]
    rb_in[z] = rb_ref[z]
    kvf[rows(z, x)] = kvpack[z]
    kvf[0] = jnp.zeros((BLK, LANES), BF16)
    kvf[nb + 1] = jnp.zeros((BLK, LANES), BF16)

    @pl.loop(1, nz)
    def _(i):
        zs = src_of(i)
        remote(qpack.at[zs], q_in.at[zs], q_send.at[zs], q_recv.at[zs], dev(zs, x)).wait_recv()
        remote(rb_ref.at[zs], rb_in.at[zs], rb_send.at[zs], rb_recv.at[zs], dev(zs, x)).wait_recv()

    to_smem = pltpu.make_async_copy(rb_in, rb_s, rbs_sem)
    to_smem.start()

    lo_b = lax.broadcasted_iota(jnp.int32, (BLK, LANES), 1) < HALF

    def spread(number):
        return jnp.broadcast_to(number, (BLK, LANES))

    for g in range(G):
        block = gb_ref[g]
        within = lax.rem(block, bd)
        tile = q_in[lax.div(block, bd * X), lax.rem(within, half_bd)]
        tile = jnp.where(spread(within) >= half_bd, swap(tile), tile)
        qc_in[x, g] = jnp.where(lo_b, tile, jnp.zeros_like(tile))

    def qc_copy(d):
        return remote(qc_in.at[x], qc_in.at[x], qc_send.at[d], qc_recv.at[x], dev(z, lax.rem(x + d, X)))

    def qc_wait(d):
        xs = lax.rem(x + d, X)
        remote(qc_in.at[xs], qc_in.at[xs], qc_send.at[d], qc_recv.at[xs], dev(z, xs)).wait_recv()

    for d in range(1, X):
        qc_copy(d).start()
    for d in range(1, X):
        qc_wait(d)

    glob_q = jnp.concatenate(
        [qc_in[lax.rem(lax.div(gb_ref[g], bd), X), g] for g in range(G)], axis=0
    )
    gout[...] = jnp.zeros_like(gout)
    stat[0] = jnp.full((G * BLK, LANES), NEG, F32)
    stat[1] = jnp.zeros((G * BLK, LANES), F32)

    def right_copy(zs):
        part = kvf.at[rows(zs, x)]
        return remote(part, part, r_send.at[zs], fl_recv.at[zs], dev(z, right))

    def left_copy(zs):
        part = kvf.at[rows(zs, x)]
        return remote(part, part, l_send.at[zs], fr_recv.at[zs], dev(z, left))

    def from_left(zs):
        part = kvf.at[rows(zs, left)]
        return remote(part, part, r_send.at[zs], fl_recv.at[zs], dev(z, left))

    def from_right(zs):
        part = kvf.at[rows(zs, right)]
        return remote(part, part, l_send.at[zs], fr_recv.at[zs], dev(z, right))

    def half_right(zs):
        part = kvf.at[rows(zs, left, 0, half_bd)]
        return remote(part, part, ha_send.at[zs], oa_recv.at[zs], dev(z, right))

    def half_left(zs):
        part = kvf.at[rows(zs, right, half_bd, half_bd)]
        return remote(part, part, hb_send.at[zs], ob_recv.at[zs], dev(z, left))

    opposite = lax.rem(x + 2, X)

    def half_a(zs):
        part = kvf.at[rows(zs, opposite, 0, half_bd)]
        return remote(part, part, ha_send.at[zs], oa_recv.at[zs], dev(z, left))

    def half_b(zs):
        part = kvf.at[rows(zs, opposite, half_bd, half_bd)]
        return remote(part, part, hb_send.at[zs], ob_recv.at[zs], dev(z, right))

    def pass_on(zs):
        from_left(zs).wait_recv()
        half_right(zs).start()
        from_right(zs).wait_recv()
        half_left(zs).start()

    @pl.loop(0, nz)
    def _(i):
        zs = src_of(i)

        @pl.when(i > 0)
        def _():
            part = kvf.at[rows(zs, x)]
            remote(part, part, kv_send.at[zs], kv_recv.at[zs], dev(zs, x)).wait_recv()

        right_copy(zs).start()
        left_copy(zs).start()
        chunk = kvf[rows(zs, x)].reshape(tok, LANES)
        scores = dot_nt(glob_q, chunk)
        old_max = stat[0]
        new_max = jnp.maximum(old_max, jnp.max(scores, axis=1, keepdims=True))
        shrink = jnp.exp2((old_max - new_max) * scale2)
        weights = jnp.exp2((scores - new_max[:, :1]) * scale2)
        stat[0] = new_max
        stat[1] = stat[1] * shrink + jnp.sum(weights, axis=1, keepdims=True)
        gout[...] = gout[...] * shrink + dot_nn(weights.astype(BF16), chunk)

        @pl.when(i > 0)
        def _():
            pass_on(src_of(i - 1))

    pass_on(src_of(nz - 1))

    lane_g = lax.broadcasted_iota(jnp.int32, (G * BLK, LANES), 1)
    gpart[x] = jnp.where(lane_g < HALF // 2, stat[0], jnp.where(lane_g < HALF, stat[1], gout[...]))

    def gp_copy(d):
        return remote(gpart.at[x], gpart.at[x], gp_send.at[d], gp_recv.at[x], dev(z, lax.rem(x + d, X)))

    def gp_wait(d):
        xs = lax.rem(x + d, X)
        remote(gpart.at[xs], gpart.at[xs], gp_send.at[d], gp_recv.at[xs], dev(z, xs)).wait_recv()

    for d in range(1, X):
        gp_copy(d).start()

    @pl.loop(0, nz)
    def _(i):
        zs = src_of(i)
        half_a(zs).wait_recv()
        half_b(zs).wait_recv()

    for d in range(1, X):
        gp_wait(d)
    top_max = functools.reduce(jnp.maximum, [gpart[c][:, :1] for c in range(X)])
    glob_total = jnp.zeros((G * BLK, 1), F32)
    glob_acc = jnp.zeros((G * BLK, LANES), F32)
    for c in range(X):
        part = gpart[c]
        factor = jnp.exp2((part[:, :1] - top_max) * scale2)
        glob_total = glob_total + part[:, HALF // 2:HALF // 2 + 1] * factor
        glob_acc = glob_acc + part * factor
    gout[...] = glob_acc / glob_total

    for g in range(G):
        gkv[g * BLK:(g + 1) * BLK, :] = kvf[1 + gb_ref[g]]
    to_smem.wait()

    key_lane = lax.broadcasted_iota(jnp.int32, (BLK, (3 + R + G) * BLK), 1)

    @pl.loop(0, nz)
    def _(i):
        zs = src_of(i)
        packed = q_in[zs].reshape(half_tok, LANES)
        zero = jnp.zeros_like(packed)
        halves = (jnp.where(lo_q, packed, zero), jnp.where(lo_q, swap(packed), zero))
        outs = []
        for j in range(bd):
            block = (zs * X + x) * bd + j
            first = (j % half_bd) * BLK
            qb = halves[j // half_bd][first:first + BLK, :]
            parts = [kvf[block + w] for w in range(3)]
            for r in range(R):
                pick = rb_s[zs, 0, j * R + r]
                parts.append(kvf[1 + pick])
            parts.append(gkv[...])
            keyval = jnp.concatenate(parts, axis=0)
            scores = dot_nt(qb, keyval)
            if j == 0:
                scores = jnp.where((key_lane < BLK) & (block == 0), NEG, scores)
            if j == bd - 1:
                outside = (key_lane >= 2 * BLK) & (key_lane < 3 * BLK) & (block == nb - 1)
                scores = jnp.where(outside, NEG, scores)
            row_max = jnp.max(scores, axis=1, keepdims=True)
            weights = jnp.exp2((scores - row_max) * scale2)
            total = jnp.sum(weights, axis=1, keepdims=True)
            mixed = dot_nn(weights.astype(BF16), keyval) / total
            for g in range(G):
                mixed = jnp.where(spread(gb_ref[g]) == block, gout[g * BLK:(g + 1) * BLK, :], mixed)
            outs.append(mixed)
        low = jnp.concatenate(outs[:half_bd], axis=0)
        high = jnp.concatenate(outs[half_bd:], axis=0)
        o_pack[zs] = jnp.where(lo_q, pltpu.roll(low, HALF, 1), high).astype(BF16)

        @pl.when(i > 0)
        def _():
            o_copy(zs).start()

    o_in[z] = o_pack[z]

    @pl.loop(1, nz)
    def _(i):
        zs = src_of(i)
        remote(o_pack.at[zs], o_in.at[zs], o_send.at[zs], o_recv.at[zs], dev(zs, x)).wait_recv()

    for p in range(nz // 2):
        cols = slice(p * LANES, (p + 1) * LANES)
        even, odd = o_in[2 * p], o_in[2 * p + 1]
        ctx_ref[:half_tok, cols] = jnp.where(lo_q, even, swap(odd))
        ctx_ref[half_tok:, cols] = jnp.where(lo_q, swap(even), odd)

    @pl.loop(1, nz)
    def _(i):
        dz = dest_of(i)
        q_copy(dz).wait_send()
        rb_copy(dz).wait_send()
        kv_copy(dz).wait_send()
        o_copy(dz).wait_send()

    @pl.loop(0, nz)
    def _(i):
        right_copy(i).wait_send()
        left_copy(i).wait_send()
        half_right(i).wait_send()
        half_left(i).wait_send()

    for d in range(1, X):
        qc_copy(d).wait_send()
        gp_copy(d).wait_send()


def per_device(queries, keys_values, random_blocks, global_blocks, out_proj):
    tokens, width = queries.shape
    bd = tokens // BLK
    nz = lax.axis_size("seq") // X
    head_dim = width // H
    assert nz == H and head_dim == HALF and bd % 2 == 0
    lists = random_blocks.transpose(1, 0, 2).reshape(H, 1, bd * R)
    lists = jnp.pad(lists, ((0, 0), (0, 7), (0, LANES - bd * R)))
    nb = nz * X * bd
    scale2 = 1.4426950408889634 * head_dim ** -0.5
    dma = pltpu.SemaphoreType.DMA
    vm = pl.BlockSpec(memory_space=pltpu.VMEM)
    half_tok = tokens // 2
    ctx = pl.pallas_call(
        functools.partial(kernel, nz, bd, scale2),
        out_shape=jax.ShapeDtypeStruct((tokens, width), BF16),
        in_specs=[pl.BlockSpec(memory_space=pltpu.SMEM), vm, vm, vm],
        out_specs=vm,
        scratch_shapes=[
            pltpu.VMEM((nz, bd // 2, BLK, LANES), BF16),
            pltpu.VMEM((nz, bd, BLK, LANES), BF16),
            pltpu.VMEM((nb + 2, BLK, LANES), BF16),
            pltpu.VMEM((nz, bd // 2, BLK, LANES), BF16),
            pltpu.VMEM((nz, 8, LANES), jnp.int32),
            pltpu.SMEM((nz, 8, LANES), jnp.int32),
            pltpu.VMEM((X, G, BLK, LANES), BF16),
            pltpu.VMEM((X, G * BLK, LANES), F32),
            pltpu.VMEM((G * BLK, LANES), F32),
            pltpu.VMEM((G * BLK, LANES), BF16),
            pltpu.VMEM((nz, half_tok, LANES), BF16),
            pltpu.VMEM((nz, half_tok, LANES), BF16),
            pltpu.VMEM((2, G * BLK, LANES), F32),
        ]
        + [dma((nz,))] * 16
        + [dma((X,))] * 4
        + [dma],
        compiler_params=pltpu.CompilerParams(
            collective_id=0, has_side_effects=True, vmem_limit_bytes=40 * 1024 * 1024
        ),
    )(global_blocks, queries, keys_values, lists)
    weights = lax.all_gather(out_proj, "seq", axis=0, tiled=True)
    return jnp.dot(ctx, weights, preferred_element_type=F32).astype(BF16)


def solution(mesh):
    placed = (
        P(("batch", "seq"), None),
        P(None, ("batch", "seq"), None),
        P(("batch", "seq"), None, None),
        P("batch"),
        P("seq", None),
    )
    return jax.shard_map(
        per_device, mesh=mesh, in_specs=placed, out_specs=P(("batch", "seq"), None), check_vma=False
    )
```

time: 1050 us -> 185 us (0.18)
  waiting for transfers between devices: 497 us -> 26.6 us
  blocking collectives: 289 us -> 0 us
  Pallas kernels: 0 us -> 137 us
  local copies, waits for them, and re-layouts: 98.8 us -> 3.72 us
  other arithmetic: 59.6 us -> 0 us
  starting transfers between devices: 33.9 us -> 0.01 us
  matrix products: 35.1 us -> 3.09 us
  loops' own time: 15.7 us -> 0 us
    psum x2 -> x0, waiting for transfers between devices: 477 us -> none  [the longest x1 380 us: broadcast(): return lax.psum(kept, axis)]
    pmax x1 -> x0, blocking collectives: 149 us -> none  [per_device(): row_max = lax.pmax(local_max, 'seq')]
    psum x1 -> x0, blocking collectives: 140 us -> none  [per_device(): glob_sum, glob_acc = lax.psum((local_sum, weighted), 'seq')]
    pallas_call x0 -> x1, Pallas kernels: none -> 137 us  [per_device(): pl.pallas_call(functools.partial(kernel, nz, bd, scale2), out_shape=jax.S...]
    gather x4 -> x0, local copies, waits for them, and re-layouts: 55.7 us -> none  [the longest x3 29.8 us: per_device(): jnp.take(returned, slot_index, axis=1)]
    dot_general x27 -> x1, matrix products: 35.1 us -> 3.09 us  [per_device(): return jnp.dot(ctx, weights, preferred_element_type=F32).astype(BF16)]
    sub x4 -> x0, other arithmetic: 28.7 us -> none  [attend(): weights = jnp.exp(scores - row_max[:, :, None])]
    all_to_all x2 -> x0, starting transfers between devices: 28.3 us -> none  [the longest x1 18.6 us: per_device(): lax.all_to_all(request.reshape(devices, capacity), 'seq', split_axis=0, c...]
  transfers between devices with their start and end apart: 7 -> 1, of which waited for: 6 -> 1; matrix products, arithmetic and copies ran while one was open for 14% -> 0% of each run, Pallas kernels for 0% -> 75%
where the time goes in v1:
time: 185 us; the launch traced here: 184 us
  Pallas kernels  137 us (74%)
  waiting for transfers between devices  26.6 us (14%)
  between operations  13.4 us (7%)
  local copies, waits for them, and re-layouts  3.72 us (2%)
  matrix products  3.09 us (2%)
    pallas_call x1, Pallas kernels, per_device(): pl.pallas_call(functools.partial(kernel, nz, bd, scale2), out_shape=jax.S...  137 us
    all_gather x1, waiting for transfers between devices, per_device(): weights = lax.all_gather(out_proj, 'seq', axis=0, tiled=True)  25.9 us
  transfers between devices with their start and end apart: 1, of which 1 were waited for; matrix products, arithmetic and copies ran while one was open for 0% of the time, Pallas kernels for 75%

profile of v1, /device:TPU:24, one launch (start us, length us, event | category | flops | bytes accessed | tf_op | source)
XLA Modules:
  0.0 184.2 jit_solution(14530293776092548546)
XLA Ops:
  6.5 0.0 all-gather.2.cloned.1.call-start
  6.5 0.7 all-gather.2.cloned.1.call-update
  7.3 0.7 copy.7
  8.0 0.1 copy.8
  8.1 0.0 copy-start
  8.1 1.2 copy-done
  9.3 0.0 copy-start.1
  9.3 1.0 copy-done.1
  10.3 0.0 copy-start.2
  10.3 0.7 copy-done.2
  11.0 137.4 %shard_map.55 = bf16[256,1024]{1,0:T(8,128)(2,1)S(1)} custom-call(s32[2]{0:T(128)S(1)} %copy-done.2, bf16[256,1024]{1,0:T(8,128)(2,1)S(1)} %copy-done.1, bf16[2,256,1024]{2,1,0:T(8,128)(2,1)S(1)} %copy-done, s32[16,8,128]{2,1,0:T(8,128)S(1)} %pad.4.rb_ref), custom_call_target="tpu_custom_call" | custom-call | tf_op jit(solution)/shard_map/pallas_call | solution.py:355
  148.3 25.9 %all-gather.2.cloned.1.call-done = bf16[1024,1024]{1,0:T(8,128)(2,1)} async-done(((bf16[16,1024]{1,0:T(8,128)(2,1)}), bf16[1024,1024]{1,0:T(8,128)(2,1)}) %all-gather.2.cloned.1.call-update) | async-done | bytes 2097168 | tf_op jit(solution)/shard_map/all_gather | solution.py:382
  174.3 3.1 %convolution_convert_fusion = bf16[256,1024]{1,0:T(8,128)(2,1)} fusion(bf16[256,1024]{1,0:T(8,128)(2,1)S(1)} %shard_map.55, bf16[1024,1024]{1,0:T(8,128)(2,1)} %all-gather.2.cloned.1.call-done), kind=kOutput, calls=%fused_computation | convolution fusion | flops 537133056 | bytes 3145728 | tf_op jit(solution)/shard_map/dot_general | solution.py:383
  (2 shorter events, 0.0 us)
Async XLA Ops:
  6.5 167.7 %all-gather.2.cloned.1.call-start = ((), (), s32[]{:S(2)}) async-start(), calls=%async_computation | async-start | bytes 2129920 | tf_op jit(solution)/shard_map/all_gather | solution.py:382
  8.1 1.2 copy-start
  9.3 1.0 copy-start.1
  10.3 0.7 copy-start.2
Sparse Core Ops, SparseCore 0:
  10.3 163.9 all-gather.1

commit v2 on v1

--- a/solution.py
+++ b/solution.py
@@ -34,11 +34,12 @@
 
 def kernel(
     nz, bd, scale2,
-    gb_ref, q_ref, kv_ref, rb_ref, ctx_ref,
+    gb_ref, rb_ref, q_hbm, kv_hbm, w_hbm, out_ref,
+    q_ref, kv_ref, w_ref, rb_out, ctx_ref, w_all,
     qpack, kvpack, kvf, q_in, rb_in, rb_s, qc_in, gpart, gout, gkv, o_pack, o_in, stat,
     q_send, q_recv, rb_send, rb_recv, kv_send, kv_recv, o_send, o_recv,
     r_send, l_send, fl_recv, fr_recv, ha_send, hb_send, oa_recv, ob_recv,
-    qc_send, qc_recv, gp_send, gp_recv, rbs_sem,
+    wz_send, wz_recv, qc_send, qc_recv, gp_send, gp_recv, wx_send, wx_recv, wb_send, wb_recv, load_sem, rbs_sem,
 ):
     tok = bd * BLK
     half_tok = tok // 2
@@ -46,6 +47,8 @@
     nb = nz * X * bd
     batch = lax.axis_index("batch")
     me = lax.axis_index("seq")
+    nk = lax.axis_size("batch")
+    cols_k = out_ref.shape[1] // nk
     z = me // X
     x = lax.rem(me, X)
     right = lax.rem(x + 1, X)
@@ -71,6 +74,13 @@
     def rows(zz, xx, first=0, count=None):
         return pl.ds(1 + (zz * X + xx) * bd + first, bd if count is None else count)
 
+    loads = [
+        pltpu.make_async_copy(src, dst, load_sem.at[n])
+        for n, (src, dst) in enumerate(((q_hbm, q_ref), (kv_hbm, kv_ref), (w_hbm, w_ref)))
+    ]
+    for load in loads:
+        load.start()
+
     barrier = pltpu.get_barrier_semaphore()
 
     @pl.loop(1, nz)
@@ -79,6 +89,19 @@
 
     for d in range(1, X):
         pl.semaphore_signal(barrier, inc=1, device_id=dev(z, lax.rem(x + d, X)), device_id_type=MESH)
+
+    @pl.loop(1, nk)
+    def _(i):
+        pl.semaphore_signal(barrier, inc=1, device_id=(lax.rem(batch + i, nk), me), device_id_type=MESH)
+
+    lane_l = lax.broadcasted_iota(jnp.int32, (nz, LANES), 1)
+    lists = jnp.zeros((nz, LANES), jnp.int32)
+    for j in range(bd):
+        for r in range(R):
+            lists = jnp.where(lane_l == j * R + r, rb_ref[j, :, r:r + 1], lists)
+    for h in range(nz):
+        rb_out[h] = lists[h:h + 1, :]
+    loads[0].wait()
 
     lo_q = lax.broadcasted_iota(jnp.int32, (half_tok, LANES), 1) < HALF
     for p in range(nz // 2):
@@ -87,13 +110,32 @@
         qpack[2 * p] = jnp.where(lo_q, top, swap(bot)).reshape(half_bd, BLK, LANES)
         qpack[2 * p + 1] = jnp.where(lo_q, swap(top), bot).reshape(half_bd, BLK, LANES)
 
-    pl.semaphore_wait(barrier, nz - 1 + X - 1)
+    loads[2].wait()
+    for kk in range(nk):
+        @pl.when(batch == kk)
+        def _():
+            w_all[kk, x, z] = w_ref[:, kk * cols_k:(kk + 1) * cols_k]
+
+    pl.semaphore_wait(barrier, nz - 1 + X - 1 + nk - 1)
 
     def q_copy(dz):
         return remote(qpack.at[dz], q_in.at[z], q_send.at[dz], q_recv.at[z], dev(dz, x))
 
     def rb_copy(dz):
-        return remote(rb_ref.at[dz], rb_in.at[z], rb_send.at[dz], rb_recv.at[z], dev(dz, x))
+        return remote(rb_out.at[dz], rb_in.at[z], rb_send.at[dz], rb_recv.at[z], dev(dz, x))
+
+    def wz_copy(dz):
+        part = w_all.at[batch, x, z]
+        return remote(part, part, wz_send.at[dz], wz_recv.at[z], dev(dz, x))
+
+    def wx_copy(d):
+        part = w_all.at[batch, x]
+        return remote(part, part, wx_send.at[d], wx_recv.at[x], dev(z, lax.rem(x + d, X)))
+
+    def wb_copy(i):
+        to = lax.rem(batch + i, nk)
+        part = w_all.at[batch]
+        return remote(part, part, wb_send.at[to], wb_recv.at[batch], (to, me))
 
     def kv_copy(dz):
         return remote(kvpack.at[dz], kvf.at[rows(z, x)], kv_send.at[dz], kv_recv.at[z], dev(dz, x))
@@ -106,7 +148,9 @@
         dz = dest_of(i)
         q_copy(dz).start()
         rb_copy(dz).start()
-
+        wz_copy(dz).start()
+
+    loads[1].wait()
     lo_t = lax.broadcasted_iota(jnp.int32, (tok, LANES), 1) < HALF
     for p in range(nz // 2):
         cols = slice(p * LANES, (p + 1) * LANES)
@@ -119,7 +163,7 @@
         kv_copy(dest_of(i)).start()
 
     q_in[z] = qpack[z]
-    rb_in[z] = rb_ref[z]
+    rb_in[z] = rb_out[z]
     kvf[rows(z, x)] = kvpack[z]
     kvf[0] = jnp.zeros((BLK, LANES), BF16)
     kvf[nb + 1] = jnp.zeros((BLK, LANES), BF16)
@@ -128,7 +172,12 @@
     def _(i):
         zs = src_of(i)
         remote(qpack.at[zs], q_in.at[zs], q_send.at[zs], q_recv.at[zs], dev(zs, x)).wait_recv()
-        remote(rb_ref.at[zs], rb_in.at[zs], rb_send.at[zs], rb_recv.at[zs], dev(zs, x)).wait_recv()
+        remote(rb_out.at[zs], rb_in.at[zs], rb_send.at[zs], rb_recv.at[zs], dev(zs, x)).wait_recv()
+        part = w_all.at[batch, x, zs]
+        remote(part, part, wz_send.at[zs], wz_recv.at[zs], dev(zs, x)).wait_recv()
+
+    for d in range(1, X):
+        wx_copy(d).start()
 
     to_smem = pltpu.make_async_copy(rb_in, rb_s, rbs_sem)
     to_smem.start()
@@ -229,7 +278,16 @@
         def _():
             pass_on(src_of(i - 1))
 
-    pass_on(src_of(nz - 1))
+        @pl.when(i == 2)
+        def _():
+            for d in range(1, X):
+                xs = lax.rem(x + d, X)
+                part = w_all.at[batch, xs]
+                remote(part, part, wx_send.at[d], wx_recv.at[xs], dev(z, xs)).wait_recv()
+
+            @pl.loop(1, nk)
+            def _(n):
+                wb_copy(n).start()
 
     lane_g = lax.broadcasted_iota(jnp.int32, (G * BLK, LANES), 1)
     gpart[x] = jnp.where(lane_g < HALF // 2, stat[0], jnp.where(lane_g < HALF, stat[1], gout[...]))
@@ -243,6 +301,7 @@
 
     for d in range(1, X):
         gp_copy(d).start()
+    pass_on(src_of(nz - 1))
 
     @pl.loop(0, nz)
     def _(i):
@@ -269,7 +328,8 @@
     key_lane = lax.broadcasted_iota(jnp.int32, (BLK, (3 + R + G) * BLK), 1)
 
     @pl.loop(0, nz)
-    def _(i):
+    def _(n):
+        i = nz - 1 - n
         zs = src_of(i)
         packed = q_in[zs].reshape(half_tok, LANES)
         zero = jnp.zeros_like(packed)
@@ -324,6 +384,7 @@
         dz = dest_of(i)
         q_copy(dz).wait_send()
         rb_copy(dz).wait_send()
+        wz_copy(dz).wait_send()
         kv_copy(dz).wait_send()
         o_copy(dz).wait_send()
 
@@ -334,7 +395,28 @@
         half_right(i).wait_send()
         half_left(i).wait_send()
 
-    for d in range(1, X):
+    @pl.loop(1, nk)
+    def _(n):
+        kk = lax.rem(batch + n, nk)
+        part = w_all.at[kk]
+        remote(part, part, wb_send.at[kk], wb_recv.at[kk], (kk, me)).wait_recv()
+
+    step = 2 * cols_k
+
+    @pl.loop(0, nk // 2)
+    def _(n):
+        pair = []
+        for kk in (2 * n, 2 * n + 1):
+            pair.append(jnp.concatenate([w_all[kk, xx, zz] for zz in range(nz) for xx in range(X)], axis=0))
+        product = dot_nn(ctx_ref[...], jnp.concatenate(pair, axis=1))
+        out_ref[:, pl.ds(pl.multiple_of(n * step, step), step)] = product.astype(BF16)
+
+    @pl.loop(1, nk)
+    def _(n):
+        wb_copy(n).wait_send()
+
+    for d in range(1, X):
+        wx_copy(d).wait_send()
         qc_copy(d).wait_send()
         gp_copy(d).wait_send()
 
@@ -345,25 +427,32 @@
     nz = lax.axis_size("seq") // X
     head_dim = width // H
     assert nz == H and head_dim == HALF and bd % 2 == 0
-    lists = random_blocks.transpose(1, 0, 2).reshape(H, 1, bd * R)
-    lists = jnp.pad(lists, ((0, 0), (0, 7), (0, LANES - bd * R)))
     nb = nz * X * bd
     scale2 = 1.4426950408889634 * head_dim ** -0.5
     dma = pltpu.SemaphoreType.DMA
     vm = pl.BlockSpec(memory_space=pltpu.VMEM)
     half_tok = tokens // 2
-    ctx = pl.pallas_call(
+    hbm = pl.BlockSpec(memory_space=pltpu.HBM)
+    nk = lax.axis_size("batch")
+    w_rows = out_proj.shape[0]
+    return pl.pallas_call(
         functools.partial(kernel, nz, bd, scale2),
         out_shape=jax.ShapeDtypeStruct((tokens, width), BF16),
-        in_specs=[pl.BlockSpec(memory_space=pltpu.SMEM), vm, vm, vm],
+        in_specs=[pl.BlockSpec(memory_space=pltpu.SMEM), vm, hbm, hbm, hbm],
         out_specs=vm,
         scratch_shapes=[
+            pltpu.VMEM((tokens, width), BF16),
+            pltpu.VMEM((2, tokens, width), BF16),
+            pltpu.VMEM((w_rows, width), BF16),
+            pltpu.VMEM((nz, 1, LANES), jnp.int32),
+            pltpu.VMEM((tokens, width), BF16),
+            pltpu.VMEM((nk, X, nz, w_rows, width // nk), BF16),
             pltpu.VMEM((nz, bd // 2, BLK, LANES), BF16),
             pltpu.VMEM((nz, bd, BLK, LANES), BF16),
             pltpu.VMEM((nb + 2, BLK, LANES), BF16),
             pltpu.VMEM((nz, bd // 2, BLK, LANES), BF16),
-            pltpu.VMEM((nz, 8, LANES), jnp.int32),
-            pltpu.SMEM((nz, 8, LANES), jnp.int32),
+            pltpu.VMEM((nz, 1, LANES), jnp.int32),
+            pltpu.SMEM((nz, 1, LANES), jnp.int32),
             pltpu.VMEM((X, G, BLK, LANES), BF16),
             pltpu.VMEM((X, G * BLK, LANES), F32),
             pltpu.VMEM((G * BLK, LANES), F32),
@@ -372,15 +461,14 @@
             pltpu.VMEM((nz, half_tok, LANES), BF16),
             pltpu.VMEM((2, G * BLK, LANES), F32),
         ]
-        + [dma((nz,))] * 16
-        + [dma((X,))] * 4
-        + [dma],
+        + [dma((nz,))] * 18
+        + [dma((X,))] * 6
+        + [dma((nk,))] * 2
+        + [dma((3,)), dma],
         compiler_params=pltpu.CompilerParams(
-            collective_id=0, has_side_effects=True, vmem_limit_bytes=40 * 1024 * 1024
+            collective_id=0, has_side_effects=True, vmem_limit_bytes=62 * 1024 * 1024
         ),
-    )(global_blocks, queries, keys_values, lists)
-    weights = lax.all_gather(out_proj, "seq", axis=0, tiled=True)
-    return jnp.dot(ctx, weights, preferred_element_type=F32).astype(BF16)
+    )(global_blocks, random_blocks, queries, keys_values, out_proj)
 
 
 def solution(mesh):

time: 185 us -> 133 us (0.72)
  waiting for transfers between devices: 26.6 us -> 0 us
  between operations: 13.4 us -> 0.01 us
  Pallas kernels: 137 us -> 128 us
  matrix products: 3.09 us -> 0 us
    all_gather x1 -> x0, waiting for transfers between devices: 25.9 us -> none  [per_device(): weights = lax.all_gather(out_proj, 'seq', axis=0, tiled=True)]
    pallas_call x1, Pallas kernels: 137 us -> 128 us  [per_device(): pl.pallas_call(functools.partial(kernel, nz, bd, scale2), out_shape=jax.S...]
    dot_general x1 -> x0, matrix products: 3.09 us -> none  [per_device(): return jnp.dot(ctx, weights, preferred_element_type=F32).astype(BF16)]
  transfers between devices with their start and end apart: 1 -> 0, of which waited for: 1 -> 0; matrix products, arithmetic and copies ran while one was open for 0% -> 0% of each run, Pallas kernels for 75% -> 0%
where the time goes in v2:
time: 133 us; the launch traced here: 131 us
  Pallas kernels  128 us (96%)
  local copies, waits for them, and re-layouts  3.27 us (2%)
    pallas_call x1, Pallas kernels, per_device(): pl.pallas_call(functools.partial(kernel, nz, bd, scale2), out_shape=jax.S...  128 us
    unnamed x2, local copies, waits for them, and re-layouts  3.27 us

profile of v2, /device:TPU:24, one launch (start us, length us, event | category | flops | bytes accessed | tf_op | source)
XLA Modules:
  0.0 131.3 jit_solution(1183948759897562643)
XLA Ops:
  0.0 1.4 %copy.6.rb_ref = s32[4,16,3]{2,1,0:T(8,128)} copy(s32[4,16,3]{1,0,2:T(4,128)} %param.7) | data formatting | bytes 1536 | tf_op args[2]
  1.4 128.1 %shard_map.55 = bf16[256,1024]{1,0:T(8,128)(2,1)} custom-call(s32[2]{0:T(128)} %gb_ref.1, s32[4,16,3]{2,1,0:T(8,128)} %copy.6.rb_ref, bf16[256,1024]{1,0:T(8,128)(2,1)} %q_hbm.1, bf16[2,256,1024]{2,1,0:T(8,128)(2,1)} %kv_hbm.1, bf16[16,1024]{1,0:T(8,128)(2,1)} %w_hbm.1), custom_call_target="tpu_custom_call" | custom-call | tf_op jit(solution)/shard_map/pallas_call | solution.py:438
  129.5 1.9 %copy.8 = bf16[256,1024]{1,0:T(8,128)(2,1)} copy(bf16[256,1024]{1,0:T(8,128)(2,1)} %shard_map.55) | data formatting | bytes 1048576

commit v3 on v2

--- a/solution.py
+++ b/solution.py
@@ -36,10 +36,10 @@
     nz, bd, scale2,
     gb_ref, rb_ref, q_hbm, kv_hbm, w_hbm, out_ref,
     q_ref, kv_ref, w_ref, rb_out, ctx_ref, w_all,
-    qpack, kvpack, kvf, q_in, rb_in, rb_s, qc_in, gpart, gout, gkv, o_pack, o_in, stat,
+    qpack, kvpack, kvf, q_in, rb_in, rb_s, cand, c_x, c_sum, c_z, c_all, gpart, gout, gkv, o_pack, o_in, stat,
     q_send, q_recv, rb_send, rb_recv, kv_send, kv_recv, o_send, o_recv,
     r_send, l_send, fl_recv, fr_recv, ha_send, hb_send, oa_recv, ob_recv,
-    wz_send, wz_recv, qc_send, qc_recv, gp_send, gp_recv, wx_send, wx_recv, wb_send, wb_recv, load_sem, rbs_sem,
+    wz_send, wz_recv, cz_send, cz_recv, cx_send, cx_recv, ca_send, gp_send, gp_recv, wx_send, wx_recv, wb_send, wb_recv, load_sem, ca_recv, rbs_sem,
 ):
     tok = bd * BLK
     half_tok = tok // 2
@@ -104,63 +104,106 @@
     loads[0].wait()
 
     lo_q = lax.broadcasted_iota(jnp.int32, (half_tok, LANES), 1) < HALF
+    lo_b = lax.broadcasted_iota(jnp.int32, (BLK, LANES), 1) < HALF
+    lo_t = lax.broadcasted_iota(jnp.int32, (tok, LANES), 1) < HALF
+
+    def spread(number):
+        return jnp.broadcast_to(number, (BLK, LANES))
+
     for p in range(nz // 2):
         cols = slice(p * LANES, (p + 1) * LANES)
-        top, bot = q_ref[:half_tok, cols], q_ref[half_tok:, cols]
-        qpack[2 * p] = jnp.where(lo_q, top, swap(bot)).reshape(half_bd, BLK, LANES)
-        qpack[2 * p + 1] = jnp.where(lo_q, swap(top), bot).reshape(half_bd, BLK, LANES)
-
-    loads[2].wait()
-    for kk in range(nk):
-        @pl.when(batch == kk)
-        def _():
-            w_all[kk, x, z] = w_ref[:, kk * cols_k:(kk + 1) * cols_k]
-
-    pl.semaphore_wait(barrier, nz - 1 + X - 1 + nk - 1)
-
-    def q_copy(dz):
-        return remote(qpack.at[dz], q_in.at[z], q_send.at[dz], q_recv.at[z], dev(dz, x))
-
-    def rb_copy(dz):
-        return remote(rb_out.at[dz], rb_in.at[z], rb_send.at[dz], rb_recv.at[z], dev(dz, x))
-
-    def wz_copy(dz):
-        part = w_all.at[batch, x, z]
-        return remote(part, part, wz_send.at[dz], wz_recv.at[z], dev(dz, x))
-
-    def wx_copy(d):
-        part = w_all.at[batch, x]
-        return remote(part, part, wx_send.at[d], wx_recv.at[x], dev(z, lax.rem(x + d, X)))
-
-    def wb_copy(i):
-        to = lax.rem(batch + i, nk)
-        part = w_all.at[batch]
-        return remote(part, part, wb_send.at[to], wb_recv.at[batch], (to, me))
-
-    def kv_copy(dz):
-        return remote(kvpack.at[dz], kvf.at[rows(z, x)], kv_send.at[dz], kv_recv.at[z], dev(dz, x))
-
-    def o_copy(dz):
-        return remote(o_pack.at[dz], o_in.at[z], o_send.at[dz], o_recv.at[z], dev(dz, x))
-
-    @pl.loop(1, nz)
-    def _(i):
-        dz = dest_of(i)
-        q_copy(dz).start()
-        rb_copy(dz).start()
-        wz_copy(dz).start()
-
+        tiles = []
+        for g in range(G):
+            tile = q_ref[lax.rem(gb_ref[g], bd), :, cols]
+            tiles.append(jnp.where(spread(lax.div(gb_ref[g], bd)) == me, tile, jnp.zeros_like(tile)))
+        cand[2 * p] = jnp.where(lo_b, tiles[0], swap(tiles[1]))
+        cand[2 * p + 1] = jnp.where(lo_b, swap(tiles[0]), tiles[1])
     loads[1].wait()
-    lo_t = lax.broadcasted_iota(jnp.int32, (tok, LANES), 1) < HALF
     for p in range(nz // 2):
         cols = slice(p * LANES, (p + 1) * LANES)
         keys, vals = kv_ref[0, :, cols], kv_ref[1, :, cols]
         kvpack[2 * p] = jnp.where(lo_t, keys, swap(vals)).reshape(bd, BLK, LANES)
         kvpack[2 * p + 1] = jnp.where(lo_t, swap(keys), vals).reshape(bd, BLK, LANES)
+    loads[2].wait()
+    for kk in range(nk):
+        @pl.when(batch == kk)
+        def _():
+            w_all[kk, x, z] = w_ref[:, kk * cols_k:(kk + 1) * cols_k]
+
+    pl.semaphore_wait(barrier, nz - 1 + X - 1 + nk - 1)
+
+    def q_copy(dz):
+        return remote(qpack.at[dz], q_in.at[z], q_send.at[dz], q_recv.at[z], dev(dz, x))
+
+    def rb_copy(dz):
+        return remote(rb_out.at[dz], rb_in.at[z], rb_send.at[dz], rb_recv.at[z], dev(dz, x))
+
+    def wz_copy(dz):
+        part = w_all.at[batch, x, z]
+        return remote(part, part, wz_send.at[dz], wz_recv.at[z], dev(dz, x))
+
+    def wx_copy(d):
+        part = w_all.at[batch, x]
+        return remote(part, part, wx_send.at[d], wx_recv.at[x], dev(z, lax.rem(x + d, X)))
+
+    def wb_copy(i):
+        to = lax.rem(batch + i, nk)
+        part = w_all.at[batch]
+        return remote(part, part, wb_send.at[to], wb_recv.at[batch], (to, me))
+
+    def kv_copy(dz):
+        return remote(kvpack.at[dz], kvf.at[rows(z, x)], kv_send.at[dz], kv_recv.at[z], dev(dz, x))
+
+    def o_copy(dz):
+        return remote(o_pack.at[dz], o_in.at[z], o_send.at[dz], o_recv.at[z], dev(dz, x))
+
+    hx = nz // X
+
+    def cx_copy(d):
+        to = lax.rem(x + d, X)
+        return remote(cand.at[pl.ds(to * hx, hx)], c_x.at[x], cx_send.at[d], cx_recv.at[x], dev(z, to))
+
+    def cz_copy(k):
+        to = x * hx + k
+        return remote(c_sum.at[k], c_z.at[z], cz_send.at[k], cz_recv.at[z], dev(to, x))
+
+    for d in range(1, X):
+        cx_copy(d).start()
+
+    @pl.loop(1, nz)
+    def _(i):
+        dz = dest_of(i)
+        rb_copy(dz).start()
+        wz_copy(dz).start()
 
     @pl.loop(1, nz)
     def _(i):
         kv_copy(dest_of(i)).start()
+
+    for p in range(nz // 2):
+        cols = slice(p * LANES, (p + 1) * LANES)
+        top = q_ref[:half_bd, :, cols].reshape(half_tok, LANES)
+        bot = q_ref[half_bd:, :, cols].reshape(half_tok, LANES)
+        qpack[2 * p] = jnp.where(lo_q, top, swap(bot)).reshape(half_bd, BLK, LANES)
+        qpack[2 * p + 1] = jnp.where(lo_q, swap(top), bot).reshape(half_bd, BLK, LANES)
+
+    c_x[x] = cand[pl.ds(x * hx, hx)]
+    for d in range(1, X):
+        xs = lax.rem(x + d, X)
+        remote(c_x.at[xs], c_x.at[xs], cx_send.at[d], cx_recv.at[xs], dev(z, xs)).wait_recv()
+    c_sum[...] = (c_x[0] + c_x[1]) + (c_x[2] + c_x[3])
+    for k in range(hx):
+        @pl.when(x * hx + k != z)
+        def _():
+            cz_copy(k).start()
+
+        @pl.when(x * hx + k == z)
+        def _():
+            c_z[z] = c_sum[k]
+
+    @pl.loop(1, nz)
+    def _(n):
+        q_copy(dest_of(nz - n)).start()
 
     q_in[z] = qpack[z]
     rb_in[z] = rb_out[z]
@@ -168,51 +211,6 @@
     kvf[0] = jnp.zeros((BLK, LANES), BF16)
     kvf[nb + 1] = jnp.zeros((BLK, LANES), BF16)
 
-    @pl.loop(1, nz)
-    def _(i):
-        zs = src_of(i)
-        remote(qpack.at[zs], q_in.at[zs], q_send.at[zs], q_recv.at[zs], dev(zs, x)).wait_recv()
-        remote(rb_out.at[zs], rb_in.at[zs], rb_send.at[zs], rb_recv.at[zs], dev(zs, x)).wait_recv()
-        part = w_all.at[batch, x, zs]
-        remote(part, part, wz_send.at[zs], wz_recv.at[zs], dev(zs, x)).wait_recv()
-
-    for d in range(1, X):
-        wx_copy(d).start()
-
-    to_smem = pltpu.make_async_copy(rb_in, rb_s, rbs_sem)
-    to_smem.start()
-
-    lo_b = lax.broadcasted_iota(jnp.int32, (BLK, LANES), 1) < HALF
-
-    def spread(number):
-        return jnp.broadcast_to(number, (BLK, LANES))
-
-    for g in range(G):
-        block = gb_ref[g]
-        within = lax.rem(block, bd)
-        tile = q_in[lax.div(block, bd * X), lax.rem(within, half_bd)]
-        tile = jnp.where(spread(within) >= half_bd, swap(tile), tile)
-        qc_in[x, g] = jnp.where(lo_b, tile, jnp.zeros_like(tile))
-
-    def qc_copy(d):
-        return remote(qc_in.at[x], qc_in.at[x], qc_send.at[d], qc_recv.at[x], dev(z, lax.rem(x + d, X)))
-
-    def qc_wait(d):
-        xs = lax.rem(x + d, X)
-        remote(qc_in.at[xs], qc_in.at[xs], qc_send.at[d], qc_recv.at[xs], dev(z, xs)).wait_recv()
-
-    for d in range(1, X):
-        qc_copy(d).start()
-    for d in range(1, X):
-        qc_wait(d)
-
-    glob_q = jnp.concatenate(
-        [qc_in[lax.rem(lax.div(gb_ref[g], bd), X), g] for g in range(G)], axis=0
-    )
-    gout[...] = jnp.zeros_like(gout)
-    stat[0] = jnp.full((G * BLK, LANES), NEG, F32)
-    stat[1] = jnp.zeros((G * BLK, LANES), F32)
-
     def right_copy(zs):
         part = kvf.at[rows(zs, x)]
         return remote(part, part, r_send.at[zs], fl_recv.at[zs], dev(z, right))
@@ -264,7 +262,78 @@
 
         right_copy(zs).start()
         left_copy(zs).start()
-        chunk = kvf[rows(zs, x)].reshape(tok, LANES)
+
+        @pl.when(i > 0)
+        def _():
+            pass_on(src_of(i - 1))
+
+        @pl.when(i == nz // 5)
+        def _():
+            @pl.loop(1, nz)
+            def _(n):
+                zw = src_of(n)
+                part = w_all.at[batch, x, zw]
+                remote(part, part, wz_send.at[zw], wz_recv.at[zw], dev(zw, x)).wait_recv()
+
+            for d in range(1, X):
+                wx_copy(d).start()
+
+        @pl.when(i == 3 * nz // 8)
+        def _():
+            for d in range(1, X):
+                xs = lax.rem(x + d, X)
+                part = w_all.at[batch, xs]
+                remote(part, part, wx_send.at[d], wx_recv.at[xs], dev(z, xs)).wait_recv()
+
+            @pl.loop(1, nk)
+            def _(n):
+                wb_copy(n).start()
+
+    pass_on(src_of(nz - 1))
+
+    @pl.loop(1, nz)
+    def _(i):
+        zs = src_of(i)
+        remote(rb_out.at[zs], rb_in.at[zs], rb_send.at[zs], rb_recv.at[zs], dev(zs, x)).wait_recv()
+
+    to_smem = pltpu.make_async_copy(rb_in, rb_s, rbs_sem)
+    to_smem.start()
+
+    holder = z // hx
+
+    def ca_copy(d):
+        to = lax.rem(x + d, X)
+        return remote(c_all, c_all, ca_send.at[d], ca_recv, dev(z, to))
+
+    @pl.when(x == holder)
+    def _():
+        @pl.loop(1, nz)
+        def _(n):
+            zs = src_of(n)
+            remote(c_z.at[zs], c_z.at[zs], cz_send.at[0], cz_recv.at[zs], dev(zs, x)).wait_recv()
+
+        total = c_z[0]
+        for zz in range(1, nz):
+            total = total + c_z[zz]
+        c_all[...] = total
+        for d in range(1, X):
+            ca_copy(d).start()
+
+    @pl.when(x != holder)
+    def _():
+        remote(c_all, c_all, ca_send.at[0], ca_recv, dev(z, holder)).wait_recv()
+
+    both = c_all[...]
+    glob_q = jnp.concatenate(
+        [jnp.where(lo_b, both, jnp.zeros_like(both)), jnp.where(lo_b, swap(both), jnp.zeros_like(both))], axis=0
+    )
+    gout[...] = jnp.zeros_like(gout)
+    stat[0] = jnp.full((G * BLK, LANES), NEG, F32)
+    stat[1] = jnp.zeros((G * BLK, LANES), F32)
+
+    @pl.loop(0, nz // 2)
+    def _(n):
+        chunk = jnp.concatenate([kvf[rows(2 * n + k, x)].reshape(tok, LANES) for k in range(2)], axis=0)
         scores = dot_nt(glob_q, chunk)
         old_max = stat[0]
         new_max = jnp.maximum(old_max, jnp.max(scores, axis=1, keepdims=True))
@@ -274,21 +343,6 @@
         stat[1] = stat[1] * shrink + jnp.sum(weights, axis=1, keepdims=True)
         gout[...] = gout[...] * shrink + dot_nn(weights.astype(BF16), chunk)
 
-        @pl.when(i > 0)
-        def _():
-            pass_on(src_of(i - 1))
-
-        @pl.when(i == 2)
-        def _():
-            for d in range(1, X):
-                xs = lax.rem(x + d, X)
-                part = w_all.at[batch, xs]
-                remote(part, part, wx_send.at[d], wx_recv.at[xs], dev(z, xs)).wait_recv()
-
-            @pl.loop(1, nk)
-            def _(n):
-                wb_copy(n).start()
-
     lane_g = lax.broadcasted_iota(jnp.int32, (G * BLK, LANES), 1)
     gpart[x] = jnp.where(lane_g < HALF // 2, stat[0], jnp.where(lane_g < HALF, stat[1], gout[...]))
 
@@ -301,7 +355,6 @@
 
     for d in range(1, X):
         gp_copy(d).start()
-    pass_on(src_of(nz - 1))
 
     @pl.loop(0, nz)
     def _(i):
@@ -331,6 +384,11 @@
     def _(n):
         i = nz - 1 - n
         zs = src_of(i)
+
+        @pl.when(i > 0)
+        def _():
+            remote(qpack.at[zs], q_in.at[zs], q_send.at[zs], q_recv.at[zs], dev(zs, x)).wait_recv()
+
         packed = q_in[zs].reshape(half_tok, LANES)
         zero = jnp.zeros_like(packed)
         halves = (jnp.where(lo_q, packed, zero), jnp.where(lo_q, swap(packed), zero))
@@ -417,8 +475,18 @@
 
     for d in range(1, X):
         wx_copy(d).wait_send()
-        qc_copy(d).wait_send()
+        cx_copy(d).wait_send()
         gp_copy(d).wait_send()
+
+    @pl.when(x == holder)
+    def _():
+        for d in range(1, X):
+            ca_copy(d).wait_send()
+
+    for k in range(hx):
+        @pl.when(x * hx + k != z)
+        def _():
+            cz_copy(k).wait_send()
 
 
 def per_device(queries, keys_values, random_blocks, global_blocks, out_proj):
@@ -441,7 +509,7 @@
         in_specs=[pl.BlockSpec(memory_space=pltpu.SMEM), vm, hbm, hbm, hbm],
         out_specs=vm,
         scratch_shapes=[
-            pltpu.VMEM((tokens, width), BF16),
+            pltpu.VMEM((bd, BLK, width), BF16),
             pltpu.VMEM((2, tokens, width), BF16),
             pltpu.VMEM((w_rows, width), BF16),
             pltpu.VMEM((nz, 1, LANES), jnp.int32),
@@ -453,7 +521,11 @@
             pltpu.VMEM((nz, bd // 2, BLK, LANES), BF16),
             pltpu.VMEM((nz, 1, LANES), jnp.int32),
             pltpu.SMEM((nz, 1, LANES), jnp.int32),
-            pltpu.VMEM((X, G, BLK, LANES), BF16),
+            pltpu.VMEM((nz, BLK, LANES), BF16),
+            pltpu.VMEM((X, nz // X, BLK, LANES), BF16),
+            pltpu.VMEM((nz // X, BLK, LANES), BF16),
+            pltpu.VMEM((nz, BLK, LANES), BF16),
+            pltpu.VMEM((BLK, LANES), BF16),
             pltpu.VMEM((X, G * BLK, LANES), F32),
             pltpu.VMEM((G * BLK, LANES), F32),
             pltpu.VMEM((G * BLK, LANES), BF16),
@@ -461,14 +533,14 @@
             pltpu.VMEM((nz, half_tok, LANES), BF16),
             pltpu.VMEM((2, G * BLK, LANES), F32),
         ]
-        + [dma((nz,))] * 18
-        + [dma((X,))] * 6
+        + [dma((nz,))] * 20
+        + [dma((X,))] * 7
         + [dma((nk,))] * 2
-        + [dma((3,)), dma],
+        + [dma((3,)), dma, dma],
         compiler_params=pltpu.CompilerParams(
             collective_id=0, has_side_effects=True, vmem_limit_bytes=62 * 1024 * 1024
         ),
-    )(global_blocks, random_blocks, queries, keys_values, out_proj)
+    )(global_blocks, random_blocks, queries.reshape(bd, BLK, width), keys_values, out_proj)
 
 
 def solution(mesh):

time: 133 us -> 129 us (0.970)
  Pallas kernels: 128 us -> 125 us
    pallas_call x1, Pallas kernels: 128 us -> 125 us  [per_device(): pl.pallas_call(functools.partial(kernel, nz, bd, scale2), out_shape=jax.S...]
where the time goes in v3:
time: 129 us; the launch traced here: 128 us
  Pallas kernels  125 us (97%)
  local copies, waits for them, and re-layouts  3.27 us (3%)
    pallas_call x1, Pallas kernels, per_device(): pl.pallas_call(functools.partial(kernel, nz, bd, scale2), out_shape=jax.S...  125 us
    unnamed x2, local copies, waits for them, and re-layouts  3.27 us

profile of v3, /device:TPU:24, one launch (start us, length us, event | category | flops | bytes accessed | tf_op | source)
XLA Modules:
  0.0 128.0 jit_solution(533140182233689310)
XLA Ops:
  0.0 1.4 %copy.6.rb_ref = s32[4,16,3]{2,1,0:T(8,128)} copy(s32[4,16,3]{1,0,2:T(4,128)} %param.7) | data formatting | bytes 1536 | tf_op args[2]
  1.4 124.7 %shard_map.55 = bf16[256,1024]{1,0:T(8,128)(2,1)} custom-call(s32[2]{0:T(128)} %gb_ref.1, s32[4,16,3]{2,1,0:T(8,128)} %copy.6.rb_ref, bf16[4,64,1024]{2,1,0:T(8,128)(2,1)} %bitcast.1, bf16[2,256,1024]{2,1,0:T(8,128)(2,1)} %kv_hbm.1, bf16[16,1024]{1,0:T(8,128)(2,1)} %w_hbm.1), custom_call_target="tpu_custom_call" | custom-call | tf_op jit(solution)/shard_map/pallas_call | solution.py:506
  126.1 1.9 %copy.8 = bf16[256,1024]{1,0:T(8,128)(2,1)} copy(bf16[256,1024]{1,0:T(8,128)(2,1)} %shard_map.55) | data formatting | bytes 1048576

commit v4 on v3

--- a/solution.py
+++ b/solution.py
@@ -35,7 +35,7 @@
 def kernel(
     nz, bd, scale2,
     gb_ref, rb_ref, q_hbm, kv_hbm, w_hbm, out_ref,
-    q_ref, kv_ref, w_ref, rb_out, ctx_ref, w_all,
+    q_ref, kv_ref, w_ref, rb_out, acc, w_all,
     qpack, kvpack, kvf, q_in, rb_in, rb_s, cand, c_x, c_sum, c_z, c_all, gpart, gout, gkv, o_pack, o_in, stat,
     q_send, q_recv, rb_send, rb_recv, kv_send, kv_recv, o_send, o_recv,
     r_send, l_send, fl_recv, fr_recv, ha_send, hb_send, oa_recv, ob_recv,
@@ -176,16 +176,9 @@
         rb_copy(dz).start()
         wz_copy(dz).start()
 
-    @pl.loop(1, nz)
+    @pl.loop(1, nz // 2 - 1)
     def _(i):
         kv_copy(dest_of(i)).start()
-
-    for p in range(nz // 2):
-        cols = slice(p * LANES, (p + 1) * LANES)
-        top = q_ref[:half_bd, :, cols].reshape(half_tok, LANES)
-        bot = q_ref[half_bd:, :, cols].reshape(half_tok, LANES)
-        qpack[2 * p] = jnp.where(lo_q, top, swap(bot)).reshape(half_bd, BLK, LANES)
-        qpack[2 * p + 1] = jnp.where(lo_q, swap(top), bot).reshape(half_bd, BLK, LANES)
 
     c_x[x] = cand[pl.ds(x * hx, hx)]
     for d in range(1, X):
@@ -201,6 +194,17 @@
         def _():
             c_z[z] = c_sum[k]
 
+    @pl.loop(nz // 2 - 1, nz)
+    def _(i):
+        kv_copy(dest_of(i)).start()
+
+    for p in range(nz // 2):
+        cols = slice(p * LANES, (p + 1) * LANES)
+        top = q_ref[:half_bd, :, cols].reshape(half_tok, LANES)
+        bot = q_ref[half_bd:, :, cols].reshape(half_tok, LANES)
+        qpack[2 * p] = jnp.where(lo_q, top, swap(bot)).reshape(half_bd, BLK, LANES)
+        qpack[2 * p + 1] = jnp.where(lo_q, swap(top), bot).reshape(half_bd, BLK, LANES)
+
     @pl.loop(1, nz)
     def _(n):
         q_copy(dest_of(nz - n)).start()
@@ -245,6 +249,16 @@
         part = kvf.at[rows(zs, opposite, half_bd, half_bd)]
         return remote(part, part, hb_send.at[zs], ob_recv.at[zs], dev(z, right))
 
+    holder = z // hx
+
+    def ca_copy(d):
+        to = lax.rem(x + d, X)
+        return remote(c_all, c_all, ca_send.at[d], ca_recv, dev(z, to))
+
+    gout[...] = jnp.zeros_like(gout)
+    stat[0] = jnp.full((G * BLK, LANES), NEG, F32)
+    stat[1] = jnp.zeros((G * BLK, LANES), F32)
+
     def pass_on(zs):
         from_left(zs).wait_recv()
         half_right(zs).start()
@@ -263,6 +277,44 @@
         right_copy(zs).start()
         left_copy(zs).start()
 
+        @pl.when(i == nz // 2)
+        def _():
+            @pl.when(x == holder)
+            def _():
+                @pl.loop(1, nz)
+                def _(n):
+                    zs = src_of(n)
+                    remote(c_z.at[zs], c_z.at[zs], cz_send.at[0], cz_recv.at[zs], dev(zs, x)).wait_recv()
+
+                total = c_z[0]
+                for zz in range(1, nz):
+                    total = total + c_z[zz]
+                c_all[...] = total
+                for d in range(1, X):
+                    ca_copy(d).start()
+
+            @pl.when(x != holder)
+            def _():
+                remote(c_all, c_all, ca_send.at[0], ca_recv, dev(z, holder)).wait_recv()
+
+        @pl.when(i >= nz // 2)
+        def _():
+            n = i - nz // 2
+            both = c_all[...]
+            glob_q = jnp.concatenate(
+                [jnp.where(lo_b, both, jnp.zeros_like(both)), jnp.where(lo_b, swap(both), jnp.zeros_like(both))], axis=0
+            )
+            chunk = jnp.concatenate([kvf[rows(src_of(2 * n + k), x)].reshape(tok, LANES) for k in range(2)], axis=0)
+            scores = dot_nt(glob_q, chunk)
+            old_max = stat[0]
+            new_max = jnp.maximum(old_max, jnp.max(scores, axis=1, keepdims=True))
+            shrink = jnp.exp2((old_max - new_max) * scale2)
+            weights = jnp.exp2((scores - new_max[:, :1]) * scale2)
+            stat[0] = new_max
+            stat[1] = stat[1] * shrink + jnp.sum(weights, axis=1, keepdims=True)
+            gout[...] = gout[...] * shrink + dot_nn(weights.astype(BF16), chunk)
+
+
         @pl.when(i > 0)
         def _():
             pass_on(src_of(i - 1))
@@ -289,60 +341,6 @@
             def _(n):
                 wb_copy(n).start()
 
-    pass_on(src_of(nz - 1))
-
-    @pl.loop(1, nz)
-    def _(i):
-        zs = src_of(i)
-        remote(rb_out.at[zs], rb_in.at[zs], rb_send.at[zs], rb_recv.at[zs], dev(zs, x)).wait_recv()
-
-    to_smem = pltpu.make_async_copy(rb_in, rb_s, rbs_sem)
-    to_smem.start()
-
-    holder = z // hx
-
-    def ca_copy(d):
-        to = lax.rem(x + d, X)
-        return remote(c_all, c_all, ca_send.at[d], ca_recv, dev(z, to))
-
-    @pl.when(x == holder)
-    def _():
-        @pl.loop(1, nz)
-        def _(n):
-            zs = src_of(n)
-            remote(c_z.at[zs], c_z.at[zs], cz_send.at[0], cz_recv.at[zs], dev(zs, x)).wait_recv()
-
-        total = c_z[0]
-        for zz in range(1, nz):
-            total = total + c_z[zz]
-        c_all[...] = total
-        for d in range(1, X):
-            ca_copy(d).start()
-
-    @pl.when(x != holder)
-    def _():
-        remote(c_all, c_all, ca_send.at[0], ca_recv, dev(z, holder)).wait_recv()
-
-    both = c_all[...]
-    glob_q = jnp.concatenate(
-        [jnp.where(lo_b, both, jnp.zeros_like(both)), jnp.where(lo_b, swap(both), jnp.zeros_like(both))], axis=0
-    )
-    gout[...] = jnp.zeros_like(gout)
-    stat[0] = jnp.full((G * BLK, LANES), NEG, F32)
-    stat[1] = jnp.zeros((G * BLK, LANES), F32)
-
-    @pl.loop(0, nz // 2)
-    def _(n):
-        chunk = jnp.concatenate([kvf[rows(2 * n + k, x)].reshape(tok, LANES) for k in range(2)], axis=0)
-        scores = dot_nt(glob_q, chunk)
-        old_max = stat[0]
-        new_max = jnp.maximum(old_max, jnp.max(scores, axis=1, keepdims=True))
-        shrink = jnp.exp2((old_max - new_max) * scale2)
-        weights = jnp.exp2((scores - new_max[:, :1]) * scale2)
-        stat[0] = new_max
-        stat[1] = stat[1] * shrink + jnp.sum(weights, axis=1, keepdims=True)
-        gout[...] = gout[...] * shrink + dot_nn(weights.astype(BF16), chunk)
-
     lane_g = lax.broadcasted_iota(jnp.int32, (G * BLK, LANES), 1)
     gpart[x] = jnp.where(lane_g < HALF // 2, stat[0], jnp.where(lane_g < HALF, stat[1], gout[...]))
 
@@ -355,6 +353,16 @@
 
     for d in range(1, X):
         gp_copy(d).start()
+    pass_on(src_of(nz - 1))
+
+    @pl.loop(1, nz)
+    def _(i):
+        zs = src_of(i)
+        remote(rb_out.at[zs], rb_in.at[zs], rb_send.at[zs], rb_recv.at[zs], dev(zs, x)).wait_recv()
+
+    to_smem = pltpu.make_async_copy(rb_in, rb_s, rbs_sem)
+    to_smem.start()
+
 
     @pl.loop(0, nz)
     def _(i):
@@ -426,16 +434,37 @@
 
     o_in[z] = o_pack[z]
 
-    @pl.loop(1, nz)
-    def _(i):
-        zs = src_of(i)
-        remote(o_pack.at[zs], o_in.at[zs], o_send.at[zs], o_recv.at[zs], dev(zs, x)).wait_recv()
-
-    for p in range(nz // 2):
-        cols = slice(p * LANES, (p + 1) * LANES)
-        even, odd = o_in[2 * p], o_in[2 * p + 1]
-        ctx_ref[:half_tok, cols] = jnp.where(lo_q, even, swap(odd))
-        ctx_ref[half_tok:, cols] = jnp.where(lo_q, swap(even), odd)
+    @pl.loop(1, nk)
+    def _(n):
+        kk = lax.rem(batch + n, nk)
+        part = w_all.at[kk]
+        remote(part, part, wb_send.at[kk], wb_recv.at[kk], (kk, me)).wait_recv()
+
+    acc[...] = jnp.zeros_like(acc)
+
+    def o_wait(h):
+        remote(o_pack.at[h], o_in.at[h], o_send.at[h], o_recv.at[h], dev(h, x)).wait_recv()
+
+    def weight_rows(h):
+        parts = [jnp.concatenate([w_all[kk, xx, h] for xx in range(X)], axis=0) for kk in range(nk)]
+        return jnp.concatenate(parts, axis=1)
+
+    @pl.loop(0, nz // 2)
+    def _(n):
+        away = nz // 2 - n
+        head_a = lax.rem(z + away, nz)
+        head_b = jnp.where(n == 0, z, lax.rem(z + nz - away, nz))
+        o_wait(head_a)
+
+        @pl.when(n > 0)
+        def _():
+            o_wait(head_b)
+
+        one, two = o_in[head_a], o_in[head_b]
+        context = jnp.concatenate([jnp.where(lo_q, one, swap(two)), jnp.where(lo_q, swap(one), two)], axis=0)
+        acc[...] += dot_nn(context, jnp.concatenate([weight_rows(head_a), weight_rows(head_b)], axis=0))
+
+    out_ref[...] = acc[...].astype(BF16)
 
     @pl.loop(1, nz)
     def _(i):
@@ -452,22 +481,6 @@
         left_copy(i).wait_send()
         half_right(i).wait_send()
         half_left(i).wait_send()
-
-    @pl.loop(1, nk)
-    def _(n):
-        kk = lax.rem(batch + n, nk)
-        part = w_all.at[kk]
-        remote(part, part, wb_send.at[kk], wb_recv.at[kk], (kk, me)).wait_recv()
-
-    step = 2 * cols_k
-
-    @pl.loop(0, nk // 2)
-    def _(n):
-        pair = []
-        for kk in (2 * n, 2 * n + 1):
-            pair.append(jnp.concatenate([w_all[kk, xx, zz] for zz in range(nz) for xx in range(X)], axis=0))
-        product = dot_nn(ctx_ref[...], jnp.concatenate(pair, axis=1))
-        out_ref[:, pl.ds(pl.multiple_of(n * step, step), step)] = product.astype(BF16)
 
     @pl.loop(1, nk)
     def _(n):
@@ -513,7 +526,7 @@
             pltpu.VMEM((2, tokens, width), BF16),
             pltpu.VMEM((w_rows, width), BF16),
             pltpu.VMEM((nz, 1, LANES), jnp.int32),
-            pltpu.VMEM((tokens, width), BF16),
+            pltpu.VMEM((tokens, width), F32),
             pltpu.VMEM((nk, X, nz, w_rows, width // nk), BF16),
             pltpu.VMEM((nz, bd // 2, BLK, LANES), BF16),
             pltpu.VMEM((nz, bd, BLK, LANES), BF16),

time: 129 us -> 128 us (level)
  no operation moved by 1% of the time
where the time goes in v4:
time: 128 us; the launch traced here: 127 us
  Pallas kernels  124 us (97%)
  local copies, waits for them, and re-layouts  3.27 us (3%)
    pallas_call x1, Pallas kernels, per_device(): pl.pallas_call(functools.partial(kernel, nz, bd, scale2), out_shape=jax.S...  124 us
    unnamed x2, local copies, waits for them, and re-layouts  3.27 us

profile of v4, /device:TPU:24, one launch (start us, length us, event | category | flops | bytes accessed | tf_op | source)
XLA Modules:
  0.0 127.3 jit_solution(12729228573367036619)
XLA Ops:
  0.0 1.4 %copy.6.rb_ref = s32[4,16,3]{2,1,0:T(8,128)} copy(s32[4,16,3]{1,0,2:T(4,128)} %param.7) | data formatting | bytes 1536 | tf_op args[2]
  1.4 124.0 %shard_map.55 = bf16[256,1024]{1,0:T(8,128)(2,1)} custom-call(s32[2]{0:T(128)} %gb_ref.1, s32[4,16,3]{2,1,0:T(8,128)} %copy.6.rb_ref, bf16[4,64,1024]{2,1,0:T(8,128)(2,1)} %bitcast.1, bf16[2,256,1024]{2,1,0:T(8,128)(2,1)} %kv_hbm.1, bf16[16,1024]{1,0:T(8,128)(2,1)} %w_hbm.1), custom_call_target="tpu_custom_call" | custom-call | tf_op jit(solution)/shard_map/pallas_call | solution.py:519
  125.4 1.9 %copy.8 = bf16[256,1024]{1,0:T(8,128)(2,1)} copy(bf16[256,1024]{1,0:T(8,128)(2,1)} %shard_map.55) | data formatting | bytes 1048576
